TPU v7x, 512 devices: a whole 4x8x8 slice. The times are simulated.
512 devices in a mesh: cube: 32 (over y_hi, z, core), sub: 16 (over y_lo, x).
Axes of the slice: x: 4, y: 8 (y_hi: 2, y_lo: 4; y = y_hi * 4 + y_lo), z: 8, core: 2. Of those that a mesh axis runs over, the one named last changes fastest.
Arguments:
- leaf_update: float32 [32, 4096, 4096], P('cube', 'sub'), may hold values from -12 to 16, as said below
- maps_low: int32 [32, 32], replicated, may hold values from 0 to 31, as said below
- maps_high: int32 [16, 32], replicated, may hold values from 0 to 31, as said below
Outputs:
- factor_low: float32 [32, 4096, 128], P('cube', 'sub')
- factor_high: float32 [32, 4096, 64], P('cube', 'sub')
Inputs may be any that keep to these rules, and one draw needn't show every extreme that they name: `leaf_update`: each of the 32 slices is symmetric positive definite. `maps_low`: each row is a permutation of the 32 tiles that keeps every tile inside its block of 2 consecutive tiles and keeps in place the tiles below 2 and those from 2 to 3. `maps_high`: each row is a permutation of the 32 tiles that keeps every tile inside its block of 2 consecutive tiles and keeps in place the tiles below 2 and those from 2 to 3.
All inputs are finite; a program needn't handle non-finite values.
Results may differ from a plain program's by a relative error of at most 0.0003.
Values sent between devices are 32-bit elements; how exact they have to be, the bound alone decides.
A program may use at most 64 MiB of HBM per device.

v0:
```python
import jax
import jax.numpy as jnp
from jax import lax
from jax.sharding import PartitionSpec as P

PW = 128
PANELS = 2


HIGHEST = lax.Precision.HIGHEST


def swapped(block, axis, bit):
    count = lax.axis_size(axis)
    route = []
    for low in range(count):
        high = low | 1 << bit
        if high != low and high < count:
            route += [(low, high), (high, low)]
    return lax.ppermute(block, axis, route)


def broadcast(value, axis, source):
    kept = jnp.where(lax.axis_index(axis) == source, value, 0).astype(value.dtype)
    return lax.psum(kept, axis)


def spread_local(child_block, tile_map, row_block, column_blocks, tile_rows):
    row_count = child_block.shape[0]
    per_block = row_count // tile_rows
    inverse = jnp.argsort(tile_map)
    blocks = inverse.shape[0] // per_block
    local_map = (
        inverse.reshape(blocks, per_block)
        - (jnp.arange(blocks, dtype=jnp.int32) * per_block)[:, None]
    )
    row_source = lax.dynamic_index_in_dim(local_map, row_block, 0, keepdims=False)
    tiled_rows = child_block.reshape(per_block, tile_rows, -1)
    moved_rows = jnp.take(tiled_rows, row_source, axis=0)
    column_count = column_blocks.shape[0]
    moved_rows = moved_rows.reshape(row_count, column_count * per_block, tile_rows)
    source = jnp.take(local_map, column_blocks, axis=0)
    flat_source = (jnp.arange(column_count, dtype=jnp.int32)[:, None] * per_block + source).reshape(
        -1
    )
    placed = jnp.take(moved_rows, flat_source, axis=1)
    return placed.reshape(row_count, column_count * row_count)


def keep_outside(positions, first_row, span):
    return (positions < first_row) | (positions >= first_row + span)


def share_panel(column, tree_level):
    for bit_number in range(tree_level + 1):
        column = column + swapped(column, "cube", bit_number)
    return column


def panel_by_panel(front_block, tree_level, member, group_size, row_index, column_index, is_last):
    row_count = front_block.shape[0]
    base_row = row_count if tree_level == 0 else 0
    factors = []
    pending = None
    for panel_step in range(PANELS):
        first_row = base_row + panel_step * PW
        root_block = first_row // row_count
        offset = first_row % row_count
        owner_member = root_block % group_size
        local_start = root_block // group_size * row_count + offset
        column = jnp.where(
            member == owner_member, front_block[:, local_start : local_start + PW], 0.0
        )
        pending = None
        column = share_panel(column, tree_level)
        is_final = is_last and panel_step == PANELS - 1
        if is_final:
            pivot_block = broadcast(column[offset : offset + PW], "sub", root_block)
            lower_factor = jnp.linalg.cholesky(pivot_block)
        else:
            pivot_block, row_panel = (
                broadcast(column[offset : offset + PW], "sub", root_block),
                broadcast(front_block[offset : offset + PW], "sub", root_block),
            )
            lower_factor = jnp.linalg.cholesky(pivot_block)
            across = jax.scipy.linalg.solve_triangular(lower_factor, row_panel, lower=True)
        factor = jax.scipy.linalg.solve_triangular(lower_factor, column.T, lower=True).T
        factors.append(factor)
        if not is_final:
            keep_rows = keep_outside(row_index, first_row, PW)
            keep_columns = keep_outside(column_index, first_row, PW)
            front_block = front_block - jnp.dot(factor, across, precision=HIGHEST)
            front_block = jnp.where(keep_rows[:, None] & keep_columns[None, :], front_block, 0.0)
    return (front_block, jnp.concatenate(factors, axis=1))


def body(leaf_update, maps_low, maps_high):
    cube_index = lax.axis_index("cube")
    sub_index = lax.axis_index("sub")
    sub_count = lax.axis_size("sub")
    child_block = leaf_update[0]
    row_count, front_order = child_block.shape
    tile_rows = front_order // maps_low.shape[1]
    row_index = sub_index * row_count + jnp.arange(row_count, dtype=jnp.int32)
    outputs = []
    for tree_level in range(2):
        group_size = 2 ** (tree_level + 1)
        half_group = group_size // 2
        tile_table = maps_low if tree_level == 0 else maps_high
        tile_map = lax.dynamic_index_in_dim(tile_table, cube_index // half_group, 0, keepdims=False)
        column_blocks = (
            jnp.arange(sub_count // half_group, dtype=jnp.int32) * half_group
            + cube_index % half_group
        )
        placed = spread_local(child_block, tile_map, sub_index, column_blocks, tile_rows)
        halves = placed.reshape(row_count, sub_count // group_size, 2, row_count)
        own_bit = cube_index // half_group % 2
        kept_half = lax.dynamic_index_in_dim(halves, own_bit, 2, keepdims=False)
        sent_half = lax.dynamic_index_in_dim(halves, 1 - own_bit, 2, keepdims=False)
        front_block = (kept_half + swapped(sent_half, "cube", tree_level)).reshape(row_count, -1)
        member = cube_index % group_size
        local_columns = jnp.arange(front_block.shape[1], dtype=jnp.int32)
        column_index = (
            local_columns // row_count * group_size + member
        ) * row_count + local_columns % row_count
        is_last = tree_level == 1
        front_block, factor = panel_by_panel(
            front_block, tree_level, member, group_size, row_index, column_index, is_last
        )
        share_width = factor.shape[1] // group_size
        outputs.append(lax.dynamic_slice_in_dim(factor, member * share_width, share_width, 1)[None])
        child_block = front_block
    return (outputs[0], outputs[1])


def solution(mesh):
    in_specs = (P("cube", "sub", None), P(), P())
    out_specs = (P("cube", "sub", None), P("cube", "sub", None))
    return jax.shard_map(body, mesh=mesh, in_specs=in_specs, out_specs=out_specs, check_vma=False)
```

profile of v0, /device:TPU:32, one launch (start us, length us, event | category | flops | bytes accessed | tf_op | source)
XLA Modules:
  0.0 894.9 jit_solution(2977196503065187289)
XLA Ops:
  7.9 1.6 sort.31
  9.8 5.0 gather_fusion.1
  14.7 4.9 copy.93
  20.4 1.6 sort.32
  22.8 6.9 copy_select_fusion
  29.7 4.9 gather_fusion.2
  34.6 5.6 copy.67
  40.6 3.9 broadcast_select_fusion
  44.5 1.8 dynamic-slice_bitcast_fusion
  46.3 1.9 collective-permute-start
  48.9 3.6 collective-permute-done
  52.5 2.6 bitcast_add_fusion
  55.1 2.0 collective-permute-start.1
  60.1 171.6 %all-reduce.14.cloned.1.call-done = (f32[128,128]{0,1:T(8,128)}, f32[128,2048]{0,1:T(8,128)}) async-done(((f32[128,128]{0,1:T(8,128)}, f32[128,2048]{0,1:T(8,128)}), (f32[128,128]{0,1:T(8,128)}, f32[128,2048]{0,1:T(8,128)})) %all-reduce.14.cloned.1.call-update) | async-done | bytes 1114128 | tf_op jit(solution)/shard_map/psum | solution.py:25
  233.6 11.7 %cholesky.74 = f32[128,128]{1,0:T(8,128)S(1)} custom-call(f32[128,128]{1,0:T(8,128)S(1)} %fusion.31), custom_call_target="Cholesky" | custom-call | tf_op jit(solution)/shard_map/jit(cholesky)/cholesky | solution.py:85
  246.6 9.8 %custom-call.17 = f32[1,128,128]{1,2,0:T(8,128)S(1)} custom-call(f32[1,128,128]{2,1,0:T(8,128)S(1)} %fusion.12), custom_call_target="InvertDiagBlocksLowerTriangular" | custom-call | tf_op jit(solution)/shard_map/jit(_solve_triangular)/triangular_solve | solution.py:87
  256.7 2.3 fusion.28
  259.0 2.4 fusion.1
  261.4 1.9 collective-permute-start.2
  265.8 167.0 %all-reduce.12.cloned.1.call-done = (f32[128,128]{0,1:T(8,128)}, f32[128,2048]{0,1:T(8,128)}) async-done(((f32[128,128]{0,1:T(8,128)}, f32[128,2048]{0,1:T(8,128)}), (f32[128,128]{0,1:T(8,128)}, f32[128,2048]{0,1:T(8,128)})) %all-reduce.12.cloned.1.call-update) | async-done | bytes 1114128 | tf_op jit(solution)/shard_map/psum | solution.py:25
  434.5 11.7 %cholesky.85 = f32[128,128]{1,0:T(8,128)S(1)} custom-call(f32[128,128]{1,0:T(8,128)S(1)} %fusion.27), custom_call_target="Cholesky" | custom-call | tf_op jit(solution)/shard_map/jit(cholesky)/cholesky | solution.py:85
  447.6 9.8 %custom-call.19 = f32[1,128,128]{1,2,0:T(8,128)S(1)} custom-call(f32[1,128,128]{2,1,0:T(8,128)S(1)} %fusion.13), custom_call_target="InvertDiagBlocksLowerTriangular" | custom-call | tf_op jit(solution)/shard_map/jit(_solve_triangular)/triangular_solve | solution.py:87
  457.7 2.3 fusion.24
  460.0 3.3 fusion
  463.4 1.9 copy.92
  465.3 2.0 gather_fusion.4
  467.3 2.0 copy.94
  470.1 2.0 gather_fusion.5
  472.1 2.9 copy.78
  475.0 1.9 broadcast_select_fusion.1
  477.1 3.6 collective-permute-start.3
  480.7 13.2 %collective-permute-done.3 = f32[256,4,256]{0,2,1:T(8,128)} collective-permute-done((f32[256,4,256]{0,2,1:T(8,128)S(1)}, f32[256,4,256]{0,2,1:T(8,128)}, u32[]{:S(2)}, u32[]{:S(2)}) %collective-permute-start.3) | collective-permute-done | bytes 1048608 | tf_op jit(solution)/shard_map/ppermute | solution.py:20
  493.9 1.4 bitcast_add_fusion.1
  495.2 1.9 collective-permute-start.4
  497.2 1.3 collective-permute-done.4
  498.5 3.6 collective-permute-start.5
  502.9 3.0 collective-permute-done.5
  506.9 164.9 %all-reduce.10.cloned.1.call-done = (f32[128,128]{0,1:T(8,128)}, f32[128,1024]{0,1:T(8,128)}) async-done(((f32[128,128]{0,1:T(8,128)}, f32[128,1024]{0,1:T(8,128)}), (f32[128,128]{0,1:T(8,128)}, f32[128,1024]{0,1:T(8,128)})) %all-reduce.10.cloned.1.call-update) | async-done | bytes 589840 | tf_op jit(solution)/shard_map/psum | solution.py:25
  673.6 11.7 %cholesky.96 = f32[128,128]{1,0:T(8,128)S(1)} custom-call(f32[128,128]{1,0:T(8,128)S(1)} %fusion.23), custom_call_target="Cholesky" | custom-call | tf_op jit(solution)/shard_map/jit(cholesky)/cholesky | solution.py:85
  687.0 9.8 %custom-call.21 = f32[1,128,128]{1,2,0:T(8,128)S(1)} custom-call(f32[1,128,128]{2,1,0:T(8,128)S(1)} %copy.82), custom_call_target="InvertDiagBlocksLowerTriangular" | custom-call | tf_op jit(solution)/shard_map/jit(_solve_triangular)/triangular_solve | solution.py:87
  697.1 1.7 fusion.20
  700.0 1.9 collective-permute-start.6
  701.9 1.3 collective-permute-done.6
  703.2 3.8 collective-permute-start.7
  707.1 3.6 collective-permute-done.7
  712.2 150.3 %all-reduce.8.cloned.1.call-done = f32[128,128]{0,1:T(8,128)} async-done(((f32[128,128]{0,1:T(8,128)}), f32[128,128]{0,1:T(8,128)}) %all-reduce.8.cloned.1.call-update) | async-done | bytes 65552 | tf_op jit(solution)/shard_map/psum | solution.py:25
  864.3 11.7 %cholesky.107 = f32[128,128]{1,0:T(8,128)S(1)} custom-call(f32[128,128]{1,0:T(8,128)S(1)} %fusion.19), custom_call_target="Cholesky" | custom-call | tf_op jit(solution)/shard_map/jit(cholesky)/cholesky | solution.py:79
  877.3 9.8 %custom-call.22 = f32[1,128,128]{1,2,0:T(8,128)S(1)} custom-call(f32[1,128,128]{2,1,0:T(8,128)S(1)} %fusion.15), custom_call_target="InvertDiagBlocksLowerTriangular" | custom-call | tf_op jit(solution)/shard_map/jit(_solve_triangular)/triangular_solve | solution.py:87
  (122 shorter events, 28.7 us)
Async XLA Ops:
  7.2 0.7 copy-start
  7.2 224.6 %all-reduce.14.cloned.1.call-start = ((), (), s32[]{:S(2)}) async-start(), calls=%async_computation.3 | async-start | bytes 2228224 | tf_op jit(solution)/shard_map/psum | solution.py:25
  46.3 6.2 collective-permute-start
  55.1 3.2 collective-permute-start.1
  59.0 373.8 %all-reduce.12.cloned.1.call-start = ((), (), s32[]{:S(2)}) async-start(), calls=%async_computation.2 | async-start | bytes 2228224 | tf_op jit(solution)/shard_map/psum | solution.py:25
  261.4 3.3 copy-start.2
  261.4 3.2 collective-permute-start.2
  265.3 194.7 %copy-start.3 = (f32[256,2048]{0,1:T(8,128)S(1)}, f32[256,2048]{0,1:T(8,128)}, u32[]{:S(2)}) copy-start(f32[256,2048]{0,1:T(8,128)} %copy-done.2) | copy-start | bytes 6291460
  265.4 406.5 %all-reduce.10.cloned.1.call-start = ((), (), s32[]{:S(2)}) async-start(), calls=%async_computation.1 | async-start | bytes 1179648 | tf_op jit(solution)/shard_map/psum | solution.py:25
  477.1 16.8 %collective-permute-start.3 = (f32[256,4,256]{0,2,1:T(8,128)S(1)}, f32[256,4,256]{0,2,1:T(8,128)}, u32[]{:S(2)}, u32[]{:S(2)}) collective-permute-start(f32[256,4,256]{0,2,1:T(8,128)S(1)} %dynamic-slice_bitcast_fusion.1), channel_id=1, source_target_pairs={{0,32},{32,0},{16,48},{48,16},{64,96},{96,64},{80,112},{112,80},{1... | collective-permute-start | bytes 3145736 | tf_op jit(solution)/shard_map/ppermute | solution.py:20
  495.2 3.2 collective-permute-start.4
  498.5 7.4 collective-permute-start.5
  506.6 355.8 %all-reduce.8.cloned.1.call-start = ((), (), s32[]{:S(2)}) async-start(), calls=%async_computation | async-start | bytes 131072 | tf_op jit(solution)/shard_map/psum | solution.py:25
  697.1 191.0 %copy-start.1 = (s32[32,32]{1,0:T(8,128)S(1)}, s32[32,32]{1,0:T(8,128)}, u32[]{:S(2)}) copy-start(s32[32,32]{1,0:T(8,128)} %param.9) | copy-start | bytes 12292
  700.0 3.2 collective-permute-start.6
  703.2 7.4 collective-permute-start.7
Sparse Core Ops, SparseCore 0:
  59.1 172.6 all-reduce.13
  265.5 167.2 all-reduce.11
  506.8 165.0 all-reduce.9
  711.5 150.9 all-reduce.7
where the time goes:
time: 901 us; the launch traced here: 895 us
  waiting for transfers between devices  680 us (75%)
  other arithmetic  122 us (14%)
  local copies, waits for them, and re-layouts  41.4 us (5%)
  starting transfers between devices  21.7 us (2%)
  between operations  14.8 us (2%)
  matrix products  14.2 us (2%)
    psum x4, waiting for transfers between devices, broadcast(): return lax.psum(kept, axis)  654 us
    another operation x12, other arithmetic, panel_by_panel(): lower_factor = jnp.linalg.cholesky(pivot_block)  49.6 us
    another operation x8, other arithmetic, panel_by_panel(): jax.scipy.linalg.solve_triangular(lower_factor, column.T, lower=True)  41.9 us
    ppermute x8, waiting for transfers between devices, swapped(): return lax.ppermute(block, axis, route)  26.4 us
    ppermute x8, starting transfers between devices, swapped(): return lax.ppermute(block, axis, route)  20.7 us
  transfers between devices with their start and end apart: 12, of which 12 were waited for; matrix products, arithmetic and copies ran while one was open for 1% of the time, Pallas kernels for 0%

commit v1 on v0

v1 whole, which is shorter than its diff:
```python
import jax
import jax.numpy as jnp
from jax import lax
from jax.experimental import pallas as pl
from jax.experimental.pallas import tpu as pltpu
from jax.sharding import PartitionSpec as P

SEP = 256
HALF = 128
GROUP = 32
HIGHEST = lax.Precision.HIGHEST
MESH = pl.DeviceIdType.MESH


def dot(a, b):
    return jnp.dot(a, b, precision=HIGHEST, preferred_element_type=jnp.float32)


def dot_nt(a, b):
    return lax.dot_general(
        a, b, (((1,), (1,)), ((), ())), precision=HIGHEST, preferred_element_type=jnp.float32
    )


def lane(x, c):
    return jnp.broadcast_to(x[:, c : c + 1], (x.shape[0], HALF))


def row(x, j):
    return jnp.broadcast_to(x[j : j + 1, :], (8, HALF))


def scaled(x, r):
    n = x.shape[0]
    return (x.reshape(n // 8, 8, HALF) * r[None]).reshape(n, HALF)


def inverse_factor(trail):
    n = trail.shape[0]
    steps = n // 8
    sublane = lax.broadcasted_iota(jnp.int32, (8, HALF), 0)
    unit = (
        lax.broadcasted_iota(jnp.int32, (n, n), 0) == lax.broadcasted_iota(jnp.int32, (n, n), 1)
    ).astype(jnp.float32)
    done = []
    head = [lane(trail[:8], j) for j in range(8)]
    for k in range(steps):
        c0 = 8 * k
        t_head, t_tail = trail[:8], trail[8:]
        u_head, u_tail = unit[:8], unit[8:]
        last = k == steps - 1
        if not last:
            tail = [lane(t_tail, c0 + j) for j in range(8)]
            ahead = [lane(t_tail[:8], c0 + 8 + j) for j in range(8)]
        pivots = None
        for j in range(8):
            pivot = row(head[j], j)
            inv = 1.0 / pivot
            for q in range(j + 1, 8):
                m = row(head[q], j) * inv
                head[q] = head[q] - head[j] * m
                if not last:
                    tail[q] = tail[q] - scaled(tail[j], m)
            below = jnp.where(sublane > j, head[j], 0.0)
            u_row = row(u_head, j) * inv
            u_head = u_head - below * u_row
            if not last:
                first = tail[j][:8]
                for q in range(8):
                    ahead[q] = ahead[q] - first * (row(first, q) * inv)
                t_row = row(t_head, j) * inv
                t_head = t_head - below * t_row
                t_tail = t_tail - scaled(tail[j], t_row)
                u_tail = u_tail - scaled(tail[j], u_row)
            pivots = pivot if pivots is None else jnp.where(sublane == j, pivot, pivots)
        done.append(u_head * lax.rsqrt(pivots))
        if not last:
            trail, unit, head = t_tail, u_tail, ahead
    return jnp.concatenate(done, axis=0)


def inverse_factor_two(block, out_ref):
    inv1 = inverse_factor(block(0, 0))
    low = dot_nt(block(1, 0), inv1)
    inv2 = inverse_factor(block(1, 1) - dot_nt(low, low))
    out_ref[:HALF, :HALF] = inv1
    out_ref[:HALF, HALF:] = jnp.zeros((HALF, HALF), jnp.float32)
    out_ref[HALF:, :HALF] = -dot(inv2, dot(low, inv1))
    out_ref[HALF:, HALF:] = inv2


def kernel(
    maps_low, maps_high, leaf, out_low, out_high,
    slab, slab_in, p_stage, x_stage, pivot, lead, inv, root, panel, schur, schur_in, child, child_in, inv_high,
    load_sem, pair_sems, p_send, p_recv, x_send, x_recv, ps_send, ps_recv, xs_send, xs_recv, z_sems,
):
    cube = lax.axis_index("cube")
    sub = lax.axis_index("sub")
    front = cube // 2
    core = cube % 2
    me = 2 * sub + core

    def peer(i):
        return (2 * front + i % 2, i // 2)

    def rows(i):
        return pl.ds(pl.multiple_of(8 * i, 8), 8)

    partner = (cube + 1 - 2 * core, sub)
    other_front = front + 1 - 2 * (front % 2)
    across = (2 * other_front + core, sub)

    load = pltpu.make_async_copy(leaf.at[0, :, pl.ds(0, 2 * SEP)], slab, load_sem)
    load.start()

    barrier = pltpu.get_barrier_semaphore()

    def greet(t, carry):
        pl.semaphore_signal(barrier, inc=1, device_id=peer((me + t) % GROUP), device_id_type=MESH)
        return carry

    lax.fori_loop(1, GROUP, greet, 0)
    pl.semaphore_signal(barrier, inc=1, device_id=across, device_id_type=MESH)
    pl.semaphore_wait(barrier, GROUP)
    load.wait()

    def p_piece(i):
        return pltpu.make_async_remote_copy(
            src_ref=slab.at[rows(i), pl.ds(SEP, SEP)], dst_ref=p_stage.at[core],
            send_sem=ps_send.at[i], recv_sem=ps_recv.at[core], device_id=peer(i), device_id_type=MESH)

    def x_piece(i):
        return pltpu.make_async_remote_copy(
            src_ref=slab.at[rows(i)], dst_ref=x_stage.at[core],
            send_sem=xs_send.at[i], recv_sem=xs_recv.at[core], device_id=peer(i), device_id_type=MESH)

    def each_peer(fn):
        def step(t, carry):
            fn((me + t) % GROUP)
            return carry

        lax.fori_loop(1, GROUP, step, 0)

    @pl.when(sub == 1)
    def _():
        each_peer(lambda i: p_piece(i).start())
        p_stage[core] = slab[rows(me), SEP:]

    @pl.when(sub == 0)
    def _():
        each_peer(lambda i: x_piece(i).start())
        x_stage[core] = slab[rows(me), :]

    def p_share(i, at):
        return pltpu.make_async_remote_copy(
            src_ref=pivot.at[rows(at)], dst_ref=pivot.at[rows(at)],
            send_sem=p_send.at[i], recv_sem=p_recv.at[at], device_id=peer(i), device_id_type=MESH)

    def x_share(i, at):
        return pltpu.make_async_remote_copy(
            src_ref=lead.at[rows(at)], dst_ref=lead.at[rows(at)],
            send_sem=x_send.at[i], recv_sem=x_recv.at[at], device_id=peer(i), device_id_type=MESH)

    def stage_wait(stage, sems, root_sub):
        for c in range(2):
            @pl.when(jnp.logical_or(sub != root_sub, core != c))
            def _():
                pltpu.make_async_remote_copy(
                    src_ref=stage.at[c], dst_ref=stage.at[c], send_sem=load_sem, recv_sem=sems.at[c],
                    device_id=peer(2 * root_sub + c), device_id_type=MESH).wait_recv()

    stage_wait(p_stage, ps_recv, 1)
    pivot[rows(me), :] = p_stage[0] + p_stage[1]
    each_peer(lambda i: p_share(i, me).start())
    stage_wait(x_stage, xs_recv, 0)
    lead[rows(me), :] = x_stage[0] + x_stage[1]
    each_peer(lambda i: x_share(i, me).start())
    pair = pltpu.make_async_remote_copy(
        src_ref=slab, dst_ref=slab_in, send_sem=pair_sems.at[0], recv_sem=pair_sems.at[1],
        device_id=partner, device_id_type=MESH)
    pair.start()

    each_peer(lambda i: p_share(i, i).wait_recv())

    def pivot_quarter(i, j):
        return pivot[i * HALF : (i + 1) * HALF, j * HALF : (j + 1) * HALF]

    inverse_factor_two(pivot_quarter, inv)
    each_peer(lambda i: x_share(i, i).wait_recv())
    root[...] = dot_nt(lead[:, SEP:], inv[...])
    schur[...] = lead[:, :SEP] - dot_nt(root[...], root[...])
    z_schur = pltpu.make_async_remote_copy(
        src_ref=schur, dst_ref=schur_in, send_sem=z_sems.at[0], recv_sem=z_sems.at[1],
        device_id=across, device_id_type=MESH)
    z_schur.start()

    pair.wait_recv()

    def tiles(ref, table, index):
        moved = jnp.full((HALF, ref.shape[1]), table[index, 2 * sub], jnp.int32) != 2 * sub
        first, second = ref[:HALF, :], ref[HALF:, :]
        return jnp.where(moved, second, first), jnp.where(moved, first, second)

    own = tiles(slab, maps_low, cube)
    theirs = tiles(slab_in, maps_low, cube + 1 - 2 * core)
    keep = (sub != 1).astype(jnp.float32)
    for half in range(2):
        both = own[half] + theirs[half]
        w = dot_nt(both[:, SEP:], inv[...])
        at = slice(half * HALF, (half + 1) * HALF)
        panel[0, at, :] = w[:, :HALF]
        panel[1, at, :] = w[:, HALF:]
        child[at, :] = (both[:, :SEP] - dot_nt(w, root[...])) * keep
    z_child = pltpu.make_async_remote_copy(
        src_ref=child, dst_ref=child_in, send_sem=z_sems.at[2], recv_sem=z_sems.at[3],
        device_id=across, device_id_type=MESH)
    z_child.start()
    out_low[0] = panel[core]

    z_schur.wait_recv()

    def schur_quarter(i, j):
        at = (slice(i * HALF, (i + 1) * HALF), slice(j * HALF, (j + 1) * HALF))
        return schur[at] + schur_in[at]

    inverse_factor_two(schur_quarter, inv_high)
    z_child.wait_recv()
    own = tiles(child, maps_high, front)
    theirs = tiles(child_in, maps_high, other_front)
    share = inv_high[pl.ds(pl.multiple_of(cube % 4 * 64, 64), 64), :]
    for half in range(2):
        out_high[0, half * HALF : (half + 1) * HALF, :] = dot_nt(own[half] + theirs[half], share)

    z_schur.wait_send()
    z_child.wait_send()
    pair.wait_send()
    each_peer(lambda i: p_share(i, me).wait_send())
    each_peer(lambda i: x_share(i, me).wait_send())

    @pl.when(sub == 1)
    def _():
        each_peer(lambda i: p_piece(i).wait_send())

    @pl.when(sub == 0)
    def _():
        each_peer(lambda i: x_piece(i).wait_send())


def body(leaf_update, maps_low, maps_high):
    f32 = jnp.float32
    dma = pltpu.SemaphoreType.DMA
    return pl.pallas_call(
        kernel,
        out_shape=(
            jax.ShapeDtypeStruct((1, SEP, HALF), f32),
            jax.ShapeDtypeStruct((1, SEP, HALF // 2), f32),
        ),
        in_specs=[
            pl.BlockSpec(memory_space=pltpu.SMEM),
            pl.BlockSpec(memory_space=pltpu.SMEM),
            pl.BlockSpec(memory_space=pl.ANY),
        ],
        out_specs=(pl.BlockSpec(memory_space=pltpu.VMEM), pl.BlockSpec(memory_space=pltpu.VMEM)),
        scratch_shapes=[
            pltpu.VMEM((SEP, 2 * SEP), f32), pltpu.VMEM((SEP, 2 * SEP), f32),
            pltpu.VMEM((2, 8, SEP), f32), pltpu.VMEM((2, 8, 2 * SEP), f32),
            pltpu.VMEM((SEP, SEP), f32), pltpu.VMEM((SEP, 2 * SEP), f32),
            pltpu.VMEM((SEP, SEP), f32), pltpu.VMEM((SEP, SEP), f32), pltpu.VMEM((2, SEP, HALF), f32),
            pltpu.VMEM((SEP, SEP), f32), pltpu.VMEM((SEP, SEP), f32),
            pltpu.VMEM((SEP, SEP), f32), pltpu.VMEM((SEP, SEP), f32), pltpu.VMEM((SEP, SEP), f32),
            dma, dma((2,)), dma((GROUP,)), dma((GROUP,)), dma((GROUP,)), dma((GROUP,)),
            dma((GROUP,)), dma((2,)), dma((GROUP,)), dma((2,)), dma((4,)),
        ],
        compiler_params=pltpu.CompilerParams(
            collective_id=0, has_side_effects=True, vmem_limit_bytes=32 * 1024 * 1024
        ),
        cost_estimate=pl.CostEstimate(flops=2_000_000_000, bytes_accessed=1_000_000, transcendentals=0),
    )(maps_low, maps_high, leaf_update)


def solution(mesh):
    in_specs = (P("cube", "sub", None), P(), P())
    out_specs = (P("cube", "sub", None), P("cube", "sub", None))
    return jax.shard_map(body, mesh=mesh, in_specs=in_specs, out_specs=out_specs, check_vma=False)
```

time: 901 us -> 60.8 us (0.07)
  the two profiles are of different devices: /device:TPU:32 before, /device:TPU:62 now
where the time goes in v1:
time: 60.8 us; the launch traced here: 60.6 us
  Pallas kernels  55 us (90%)
  local copies, waits for them, and re-layouts  4.96 us (8%)
  between operations  0.65 us (1%)
    pallas_call x1, Pallas kernels, body(): pl.pallas_call(kernel, out_shape=(jax.ShapeDtypeStruct((1, SEP, HALF), f3...  55 us
    unnamed x7, local copies, waits for them, and re-layouts  4.25 us

profile of v1, /device:TPU:62, one launch (start us, length us, event | category | flops | bytes accessed | tf_op | source)
XLA Modules:
  0.0 60.6 jit_solution(8573926478432017479)
XLA Ops:
  0.6 0.0 copy-start
  0.6 2.2 %copy-done = f32[1,256,4096]{2,1,0:T(8,128)S(1)} copy-done((f32[1,256,4096]{2,1,0:T(8,128)S(1)}, f32[1,256,4096]{2,1,0:T(8,128)}, u32[]{:S(2)}) %copy-start) | copy-done | bytes 4194328
  2.8 0.0 copy-start.1
  2.8 0.7 %copy-done.1 = s32[32,32]{1,0:T(8,128)S(1)} copy-done((s32[32,32]{1,0:T(8,128)S(1)}, s32[32,32]{1,0:T(8,128)}, u32[]{:S(2)}) %copy-start.1) | copy-done | bytes 4120
  3.5 0.0 copy-start.2
  3.5 0.7 %copy-done.2 = s32[16,32]{1,0:T(8,128)S(1)} copy-done((s32[16,32]{1,0:T(8,128)S(1)}, s32[16,32]{1,0:T(8,128)}, u32[]{:S(2)}) %copy-start.2) | copy-done | bytes 2072
  4.2 55.0 %shard_map.50 = (f32[1,256,128]{2,1,0:T(8,128)S(1)}, f32[1,256,64]{2,1,0:T(8,128)S(1)}) custom-call(s32[32,32]{1,0:T(8,128)S(1)} %copy-done.1, s32[16,32]{1,0:T(8,128)S(1)} %copy-done.2, f32[1,256,4096]{2,1,0:T(8,128)S(1)} %copy-done), custom_call_target="tpu_custom_call" | custom-call | flops 2000000000 | bytes 1000000 | tf_op jit(solution)/shard_map/pallas_call | solution.py:252
  59.2 0.7 %copy.5 = f32[1,256,64]{1,2,0:T(8,128)} copy(f32[1,256,64]{2,1,0:T(8,128)S(1)} %get-tuple-element.3) | data formatting | bytes 131072 | tf_op jit(solution)/shard_map/pallas_call | solution.py:252
  59.9 0.7 %copy.7 = f32[1,256,128]{2,1,0:T(8,128)} copy(f32[1,256,128]{2,1,0:T(8,128)S(1)} %get-tuple-element.6) | data formatting | bytes 262144
Async XLA Ops:
  0.6 2.2 %copy-start = (f32[1,256,4096]{2,1,0:T(8,128)S(1)}, f32[1,256,4096]{2,1,0:T(8,128)}, u32[]{:S(2)}) copy-start(f32[1,256,4096]{2,1,0:T(8,128)} %leaf.1) | copy-start | bytes 12582916
  2.8 0.7 %copy-start.1 = (s32[32,32]{1,0:T(8,128)S(1)}, s32[32,32]{1,0:T(8,128)}, u32[]{:S(2)}) copy-start(s32[32,32]{1,0:T(8,128)} %maps_low.1) | copy-start | bytes 12292
  3.5 0.7 %copy-start.2 = (s32[16,32]{1,0:T(8,128)S(1)}, s32[16,32]{1,0:T(8,128)}, u32[]{:S(2)}) copy-start(s32[16,32]{1,0:T(8,128)} %maps_high.1) | copy-start | bytes 6148

commit v2 on v1

v2 whole, which is shorter than its diff:
```python
import jax
import jax.numpy as jnp
from jax import lax
from jax.experimental import pallas as pl
from jax.experimental.pallas import tpu as pltpu
from jax.sharding import PartitionSpec as P

SEP = 256
HALF = 128
BLOCKS = 16
HIGHEST = lax.Precision.HIGHEST
MESH = pl.DeviceIdType.MESH


def dot(a, b):
    return jnp.dot(a, b, precision=HIGHEST, preferred_element_type=jnp.float32)


def dot_nt(a, b):
    return lax.dot_general(
        a, b, (((1,), (1,)), ((), ())), precision=HIGHEST, preferred_element_type=jnp.float32
    )


def lane(x, c):
    return jnp.broadcast_to(x[:, c : c + 1], (x.shape[0], HALF))


def row(x, j):
    return jnp.broadcast_to(x[j : j + 1, :], (8, HALF))


def scaled(x, r):
    n = x.shape[0]
    return (x.reshape(n // 8, 8, HALF) * r[None]).reshape(n, HALF)


def inverse_factor(trail):
    n = trail.shape[0]
    steps = n // 8
    sublane = lax.broadcasted_iota(jnp.int32, (8, HALF), 0)
    unit = (
        lax.broadcasted_iota(jnp.int32, (n, n), 0) == lax.broadcasted_iota(jnp.int32, (n, n), 1)
    ).astype(jnp.float32)
    done = []
    head = [lane(trail[:8], j) for j in range(8)]
    for k in range(steps):
        c0 = 8 * k
        t_head, t_tail = trail[:8], trail[8:]
        u_head, u_tail = unit[:8], unit[8:]
        last = k == steps - 1
        if not last:
            tail = [lane(t_tail, c0 + j) for j in range(8)]
            ahead = [lane(t_tail[:8], c0 + 8 + j) for j in range(8)]
        pivots = None
        for j in range(8):
            pivot = row(head[j], j)
            inv = 1.0 / pivot
            for q in range(j + 1, 8):
                m = row(head[q], j) * inv
                head[q] = head[q] - head[j] * m
                if not last:
                    tail[q] = tail[q] - scaled(tail[j], m)
            below = jnp.where(sublane > j, head[j], 0.0)
            u_row = row(u_head, j) * inv
            u_head = u_head - below * u_row
            if not last:
                first = tail[j][:8]
                for q in range(8):
                    ahead[q] = ahead[q] - first * (row(first, q) * inv)
                t_row = row(t_head, j) * inv
                t_head = t_head - below * t_row
                t_tail = t_tail - scaled(tail[j], t_row)
                u_tail = u_tail - scaled(tail[j], u_row)
            pivots = pivot if pivots is None else jnp.where(sublane == j, pivot, pivots)
        done.append(u_head * lax.rsqrt(pivots))
        if not last:
            trail, unit, head = t_tail, u_tail, ahead
    return jnp.concatenate(done, axis=0)


def inverse_pair(first, second, out_ref):
    inv1 = inverse_factor(first())
    below = second()
    low = dot_nt(below[:, :HALF], inv1)
    inv2 = inverse_factor(below[:, HALF:] - dot_nt(low, low))
    out_ref[:HALF, :HALF] = inv1
    out_ref[:HALF, HALF:] = jnp.zeros((HALF, HALF), jnp.float32)
    out_ref[HALF:, :HALF] = -dot(inv2, dot(low, inv1))
    out_ref[HALF:, HALF:] = inv2


def kernel(
    maps_low, maps_high, leaf, out_low, out_high,
    slab, slab_in, front, p1, p2, lead, inv, root, root_in, panel, c1, c2, child, inv_high,
    low_table, high_table, table_sems, load_sems, pair_sems,
    p1_cut, p1_send, p1_recv, p2_cut, p2_send, p2_recv, lead_cut, lead_send, lead_recv,
    root_sems, c1_send, c1_recv, c2_send, c2_recv, child_send, child_recv,
):
    cube = lax.axis_index("cube")
    sub = lax.axis_index("sub")
    node = cube // 2
    core = cube % 2
    upper = node % 2
    other = node + 1 - 2 * upper
    partner = (cube + 1 - 2 * core, sub)
    across = (2 * other + core, sub)
    diagonal = (2 * other + 1 - core, sub)
    later, sooner = pl.ds(SEP, SEP), pl.ds(0, SEP)

    def remote(src, dst, send_sem, recv_sem, device):
        return pltpu.make_async_remote_copy(
            src_ref=src, dst_ref=dst, send_sem=send_sem, recv_sem=recv_sem, device_id=device, device_id_type=MESH
        )

    def rows(i, base=0):
        return pl.ds(pl.multiple_of(base + 8 * i, 8), 8)

    def each_peer(fn):
        def step(t, carry):
            fn((sub + t) % BLOCKS)
            return carry

        lax.fori_loop(1, BLOCKS, step, 0)

    loads = [
        pltpu.make_async_copy(leaf.at[0, :, cols], slab.at[:, cols], load_sems.at[i])
        for i, cols in enumerate((later, sooner))
    ]
    tables = [
        pltpu.make_async_copy(maps_low, low_table, table_sems.at[0]),
        pltpu.make_async_copy(maps_high, high_table, table_sems.at[1]),
    ]
    for copy in loads + tables:
        copy.start()

    barrier = pltpu.get_barrier_semaphore()

    def greet(device):
        pl.semaphore_signal(barrier, inc=1, device_id=device, device_id_type=MESH)

    for device in (partner, across, diagonal):
        greet(device)
    each_peer(lambda i: greet((cube, i)))
    for copy in tables + loads:
        copy.wait()
    pl.semaphore_wait(barrier, BLOCKS + 2)

    pairs = [
        remote(slab.at[:, cols], slab_in.at[:, cols], pair_sems.at[0, i], pair_sems.at[1, i], partner)
        for i, cols in enumerate((later, sooner))
    ]
    for copy in pairs:
        copy.start()

    def tiles(block, table, index):
        moved = jnp.full((HALF, block.shape[1]), table[index, 2 * sub], jnp.int32) != 2 * sub
        first, second = block[:HALF, :], block[HALF:, :]
        return jnp.where(moved, second, first), jnp.where(moved, first, second)

    def extend_add(cols):
        own = tiles(slab[:, cols], low_table, cube)
        theirs = tiles(slab_in[:, cols], low_table, cube + 1 - 2 * core)
        front[:HALF, cols] = own[0] + theirs[0]
        front[HALF:, cols] = own[1] + theirs[1]

    def p1_piece(i):
        return remote(front.at[rows(i), pl.ds(SEP, HALF)], p1.at[rows(i)], p1_cut.at[i], p1_recv.at[i], (cube, i))

    def p2_piece(i):
        return remote(front.at[rows(i, HALF), later], p2.at[rows(i)], p2_cut.at[i], p2_recv.at[i], (cube, i))

    def lead_piece(i):
        return remote(
            front.at[rows(i, core * HALF)], lead.at[rows(i)], lead_cut.at[i], lead_recv.at[i], (cube, i)
        )

    def share(block, send, recv, at, i):
        return remote(block.at[rows(at)], block.at[rows(at)], send.at[i], recv.at[at], (cube, i))

    def pass_on(block, send, recv, owner):
        @pl.when(sub != owner)
        def _():
            share(block, send, recv, sub, owner).wait_recv()

        each_peer(lambda i: share(block, send, recv, sub, i).start())

    def gathered(block, send, recv):
        each_peer(lambda i: share(block, send, recv, i, i).wait_recv())

    pairs[0].wait_recv()
    extend_add(slice(SEP, 2 * SEP))

    @pl.when(sub == 1)
    def _():
        each_peer(lambda i: p1_piece(i).start())
        each_peer(lambda i: p2_piece(i).start())
        p1[rows(sub), :] = front[rows(sub), SEP : SEP + HALF]
        p2[rows(sub), :] = front[rows(sub, HALF), SEP:]

    pairs[1].wait_recv()
    extend_add(slice(0, SEP))

    @pl.when(sub == 0)
    def _():
        each_peer(lambda i: lead_piece(i).start())
        lead[rows(sub), :] = front[rows(sub, core * HALF), :]

    pass_on(p1, p1_send, p1_recv, 1)
    pass_on(p2, p2_send, p2_recv, 1)
    pass_on(lead, lead_send, lead_recv, 0)

    def p1_block():
        gathered(p1, p1_send, p1_recv)
        return p1[...]

    def p2_block():
        gathered(p2, p2_send, p2_recv)
        return p2[...]

    inverse_pair(p1_block, p2_block, inv)
    gathered(lead, lead_send, lead_recv)
    root[...] = dot_nt(lead[:, SEP:], inv[...])
    root_copy = remote(root, root_in, root_sems.at[0], root_sems.at[1], partner)
    c1_copies = [
        remote(c1.at[0], c1.at[slot], c1_send.at[i], c1_recv.at[slot], device)
        for i, (slot, device) in enumerate(((0, partner), (1, across), (1, diagonal)))
    ]
    c2_copies = [
        remote(c2.at[0], c2.at[slot], c2_send.at[i], c2_recv.at[slot], device)
        for i, (slot, device) in enumerate(((0, partner), (1, across), (1, diagonal)))
    ]

    @pl.when(core == 0)
    def _():
        root_copy.start()
        c1[0] = lead[:, :HALF] - dot_nt(root[...], root[...])
        for copy in c1_copies:
            copy.start()

    @pl.when(core == 1)
    def _():
        c2[0, :, HALF:] = lead[:, HALF:SEP] - dot_nt(root[...], root[...])
        root_copy.wait_recv()
        c2[0, :, :HALF] = lead[:, :HALF] - dot_nt(root[...], root_in[...])
        for copy in c2_copies:
            copy.start()

    keep = (sub != 1).astype(jnp.float32)
    w = dot_nt(front[:, SEP:], inv[...])
    panel[0] = w[:, :HALF]
    panel[1] = w[:, HALF:]
    out_low[0] = panel[core]
    own_columns = front[:, pl.ds(pl.multiple_of(core * HALF, HALF), HALF)]
    child[core] = (own_columns - dot_nt(w, root[...])) * keep
    mine, theirs = child.at[core], child.at[2 + core]
    child_copies = [
        remote(mine, mine, child_send.at[0], child_recv.at[core], partner),
        remote(mine, theirs, child_send.at[1], child_recv.at[2 + core], across),
        remote(mine, theirs, child_send.at[2], child_recv.at[2 + core], diagonal),
    ]
    sent = [jnp.logical_or(core == 0, upper == 1), *[jnp.logical_or(core == 0, upper == 0)] * 2]
    for copy, wanted in zip(child_copies, sent):
        pl.when(wanted)(copy.start)

    def c1_block():
        @pl.when(core == 1)
        def _():
            c1_copies[0].wait_recv()

        c1_copies[1].wait_recv()
        return c1[0] + c1[1]

    def c2_block():
        @pl.when(core == 0)
        def _():
            c2_copies[0].wait_recv()

        c2_copies[1].wait_recv()
        return c2[0] + c2[1]

    inverse_pair(c1_block, c2_block, inv_high)

    def child_wait(slot):
        remote(child.at[slot], child.at[slot], child_send.at[0], child_recv.at[slot], partner).wait_recv()

    def high_columns(half):
        own = tiles(child[half], high_table, node)
        theirs = tiles(child[2 + half], high_table, other)
        return jnp.concatenate([own[0] + theirs[0], own[1] + theirs[1]], axis=0)

    pl.when(core == 1)(lambda: child_wait(0))
    child_wait(2)
    mine = pl.ds(pl.multiple_of(cube % 4 * 64, 64), 64)
    out_high[...] = dot_nt(inv_high[mine, :HALF], high_columns(0))

    @pl.when(upper == 1)
    def _():
        pl.when(core == 0)(lambda: child_wait(1))
        child_wait(3)
        out_high[...] = out_high[...] + dot_nt(inv_high[mine, HALF:], high_columns(1))

    for copy in pairs:
        copy.wait_send()
    for block, send, recv in ((p1, p1_send, p1_recv), (p2, p2_send, p2_recv), (lead, lead_send, lead_recv)):
        each_peer(lambda i: share(block, send, recv, sub, i).wait_send())

    @pl.when(sub == 1)
    def _():
        each_peer(lambda i: p1_piece(i).wait_send())
        each_peer(lambda i: p2_piece(i).wait_send())

    @pl.when(sub == 0)
    def _():
        each_peer(lambda i: lead_piece(i).wait_send())

    @pl.when(core == 0)
    def _():
        root_copy.wait_send()
        for copy in c1_copies:
            copy.wait_send()

    @pl.when(core == 1)
    def _():
        for copy in c2_copies:
            copy.wait_send()

    for copy, wanted in zip(child_copies, sent):
        pl.when(wanted)(copy.wait_send)


def body(leaf_update, maps_low, maps_high):
    dma = pltpu.SemaphoreType.DMA

    def vmem(*shape):
        return pltpu.VMEM(shape, jnp.float32)

    low, high = pl.pallas_call(
        kernel,
        out_shape=(
            jax.ShapeDtypeStruct((1, SEP, HALF), jnp.float32),
            jax.ShapeDtypeStruct((HALF // 2, SEP), jnp.float32),
        ),
        in_specs=[pl.BlockSpec(memory_space=pl.ANY)] * 3,
        out_specs=(pl.BlockSpec(memory_space=pltpu.VMEM), pl.BlockSpec(memory_space=pltpu.VMEM)),
        scratch_shapes=[
            vmem(SEP, 2 * SEP), vmem(SEP, 2 * SEP), vmem(SEP, 2 * SEP),
            vmem(HALF, HALF), vmem(HALF, SEP), vmem(HALF, 2 * SEP),
            vmem(SEP, SEP), vmem(HALF, SEP), vmem(HALF, SEP), vmem(2, SEP, HALF),
            vmem(2, HALF, HALF), vmem(2, HALF, SEP), vmem(4, SEP, HALF), vmem(SEP, SEP),
            pltpu.SMEM((32, 32), jnp.int32), pltpu.SMEM((16, 32), jnp.int32), dma((2,)), dma((2,)), dma((2, 2)),
            *[dma((BLOCKS,))] * 9,
            dma((2,)), dma((3,)), dma((2,)), dma((3,)), dma((2,)), dma((3,)), dma((4,)),
        ],
        compiler_params=pltpu.CompilerParams(
            collective_id=0, has_side_effects=True, vmem_limit_bytes=64 * 1024 * 1024
        ),
        cost_estimate=pl.CostEstimate(flops=2_000_000_000, bytes_accessed=1_000_000, transcendentals=0),
    )(maps_low, maps_high, leaf_update)
    return low, high.T[None]


def solution(mesh):
    in_specs = (P("cube", "sub", None), P(), P())
    out_specs = (P("cube", "sub", None), P("cube", "sub", None))
    return jax.shard_map(body, mesh=mesh, in_specs=in_specs, out_specs=out_specs, check_vma=False)
```

time: 60.8 us -> 47.3 us (0.78)
  the two profiles are of different devices: /device:TPU:62 before, /device:TPU:1 now
where the time goes in v2:
time: 47.3 us; the launch traced here: 47.1 us
  Pallas kernels  43.5 us (92%)
  local copies, waits for them, and re-layouts  3.04 us (6%)
  between operations  0.64 us (1%)
    pallas_call x1, Pallas kernels, body(): pl.pallas_call(kernel, out_shape=(jax.ShapeDtypeStruct((1, SEP, HALF), jn...  43.5 us
    unnamed x2, local copies, waits for them, and re-layouts  3.04 us

profile of v2, /device:TPU:1, one launch (start us, length us, event | category | flops | bytes accessed | tf_op | source)
XLA Modules:
  0.0 47.1 jit_solution(9946448789288687195)
XLA Ops:
  0.6 43.5 %shard_map.50 = (f32[1,256,128]{2,1,0:T(8,128)}, f32[64,256]{1,0:T(8,128)}) custom-call(s32[32,32]{1,0:T(8,128)} %maps_low.1, s32[16,32]{1,0:T(8,128)} %maps_high.1, f32[1,256,4096]{2,1,0:T(8,128)} %leaf.1), custom_call_target="tpu_custom_call" | custom-call | flops 2000000000 | bytes 1000000 | tf_op jit(solution)/shard_map/pallas_call | solution.py:338
  44.1 1.6 %copy.7 = f32[1,256,128]{2,1,0:T(8,128)} copy(f32[1,256,128]{2,1,0:T(8,128)} %get-tuple-element.8) | data formatting | bytes 262144
  45.7 1.5 %copy.8 = f32[1,256,64]{1,2,0:T(8,128)} copy(f32[1,256,64]{1,2,0:T(8,128)} %bitcast.3) | data formatting | bytes 131072

commit v3 on v2

v3 whole, which is shorter than its diff:
```python
import jax
import jax.numpy as jnp
from jax import lax
from jax.experimental import pallas as pl
from jax.experimental.pallas import tpu as pltpu
from jax.sharding import PartitionSpec as P

SEP = 256
HALF = 128
BLOCKS = 16
BAND = 4
HOOK = 10
HIGHEST = lax.Precision.HIGHEST
MESH = pl.DeviceIdType.MESH


def dot(a, b):
    return jnp.dot(a, b, precision=HIGHEST, preferred_element_type=jnp.float32)


def dot_nt(a, b):
    return lax.dot_general(
        a, b, (((1,), (1,)), ((), ())), precision=HIGHEST, preferred_element_type=jnp.float32
    )


def pieces(x):
    high = x.astype(jnp.bfloat16)
    rest = x - high.astype(jnp.float32)
    mid = rest.astype(jnp.bfloat16)
    return high, mid, (rest - mid.astype(jnp.float32)).astype(jnp.bfloat16)


def stacked(a, b, a_axis, b_axis):
    ah, am, al = pieces(a)
    bh, bm, bl = pieces(b)
    return lax.dot_general(
        jnp.concatenate([ah, ah, am, am, ah, al], axis=a_axis),
        jnp.concatenate([bh, bm, bh, bm, bl, bh], axis=b_axis),
        (((a_axis,), (b_axis,)), ((), ())),
        preferred_element_type=jnp.float32,
    )


def nt(a, b):
    return stacked(a, b, 1, 1)


def lane(x, c):
    return jnp.broadcast_to(x[:, c : c + 1], (x.shape[0], HALF))


def row(x, j):
    return jnp.broadcast_to(x[j : j + 1, :], (8, HALF))


def scaled(x, r):
    n = x.shape[0]
    return (x.reshape(n // 8, 8, HALF) * r[None]).reshape(n, HALF)


def inverse_factor(block, hook_at=None, hook=None):
    n = block.shape[0]
    steps = n // 8
    sublane = lax.broadcasted_iota(jnp.int32, (8, HALF), 0)
    eye = (
        lax.broadcasted_iota(jnp.int32, (n, n), 0) == lax.broadcasted_iota(jnp.int32, (n, n), 1)
    ).astype(jnp.float32)
    near = 8 * (BAND + 1)
    trail, far = block[:near], block[near:]
    unit, far_unit = eye[:near], eye[near:]
    done = []
    head = [lane(trail[:8], j) for j in range(8)]
    for k in range(steps):
        if hook is not None and k == hook_at:
            hook()
        c0 = 8 * k
        t_head, t_tail = trail[:8], trail[8:]
        u_head, u_tail = unit[:8], unit[8:]
        last = k == steps - 1
        if k % BAND == 0:
            band_rows, band_unit = [], []
        if not last:
            tail = [lane(t_tail, c0 + j) for j in range(8)]
            ahead = [lane(t_tail[:8], c0 + 8 + j) for j in range(8)]
        pivots = None
        for j in range(8):
            pivot = row(head[j], j)
            if j % 2 == 0:
                inv = 1.0 / pivot
                beside = row(head[j + 1], j)
                inv_next = pivot * (1.0 / (pivot * row(head[j + 1], j + 1) - beside * beside))
            else:
                inv = inv_next
            head_inv = head[j] * inv
            for q in range(j + 1, 8):
                m = row(head[q], j) * inv if q <= j + 2 else row(head_inv, q)
                head[q] = head[q] - head[j] * m
                if not last:
                    tail[q] = tail[q] - scaled(tail[j], m)
            below = jnp.where(sublane > j, head[j], 0.0)
            u_row = row(u_head, j) * inv
            u_head = u_head - below * u_row
            if not last:
                first = tail[j][:8]
                first_inv = first * inv
                for q in range(8):
                    ahead[q] = ahead[q] - first * row(first_inv, q)
                t_row = row(t_head, j) * inv
                t_head = t_head - below * t_row
                t_tail = t_tail - scaled(tail[j], t_row)
                u_tail = u_tail - scaled(tail[j], u_row)
            pivots = pivot if pivots is None else jnp.where(sublane == j, pivot, pivots)
        scale = lax.rsqrt(pivots)
        done.append(u_head * scale)
        if last:
            break
        band_rows.append(t_head * scale)
        band_unit.append(done[-1])
        trail, unit, head = t_tail, u_tail, ahead
        if k % BAND == BAND - 1 and far is not None:
            top = n - far.shape[0]
            rows_done = jnp.concatenate(band_rows, axis=0)
            ahead_rows = rows_done[:, top:]
            far = far - stacked(ahead_rows, rows_done, 0, 0)
            far_unit = far_unit - stacked(ahead_rows, jnp.concatenate(band_unit, axis=0), 0, 0)
            take = min(8 * BAND, n - top)
            trail = jnp.concatenate([trail, far[:take]], axis=0)
            unit = jnp.concatenate([unit, far_unit[:take]], axis=0)
            far, far_unit = (far[take:], far_unit[take:]) if top + take < n else (None, None)
    return jnp.concatenate(done, axis=0)


def kernel(
    maps_low, maps_high, leaf, out_low, out_high,
    slab, slab_in, front, p1, p2, lead, inv, root, root_in, panel, c1, c2, q2, child, high, inv_high,
    low_table, high_table, table_sems, load_sems, pair_sems,
    p1_cut, p2_cut, lead_cut, gather_send, gather_recv, piece_recv,
    root_sems, c1_send, c1_recv, c2_sems, q2_sems, child_send, child_recv, high_sems,
):
    cube = lax.axis_index("cube")
    sub = lax.axis_index("sub")
    node = cube // 2
    core = cube % 2
    upper = node % 2
    other = node + 1 - 2 * upper
    partner = (cube + 1 - 2 * core, sub)
    across = (2 * other + core, sub)
    diagonal = (2 * other + 1 - core, sub)
    parts = ((SEP, HALF), (SEP + HALF, HALF), (0, SEP))

    def remote(src, dst, send_sem, recv_sem, device):
        return pltpu.make_async_remote_copy(
            src_ref=src, dst_ref=dst, send_sem=send_sem, recv_sem=recv_sem, device_id=device, device_id_type=MESH
        )

    def rows(i, base=0):
        return pl.ds(pl.multiple_of(base + 8 * i, 8), 8)

    def each_peer(fn):
        def step(t, carry):
            fn((sub + t) % BLOCKS)
            return carry

        lax.fori_loop(1, BLOCKS, step, 0)

    loads = [
        pltpu.make_async_copy(leaf.at[0, :, pl.ds(*part)], slab.at[:, pl.ds(*part)], load_sems.at[i])
        for i, part in enumerate(parts)
    ]
    tables = [
        pltpu.make_async_copy(maps_low, low_table, table_sems.at[0]),
        pltpu.make_async_copy(maps_high, high_table, table_sems.at[1]),
    ]
    for copy in loads + tables:
        copy.start()

    barrier = pltpu.get_barrier_semaphore()

    def greet(device):
        pl.semaphore_signal(barrier, inc=1, device_id=device, device_id_type=MESH)

    for device in (partner, across, diagonal):
        greet(device)
    each_peer(lambda i: greet((cube, i)))
    for copy in tables + loads:
        copy.wait()
    pl.semaphore_wait(barrier, BLOCKS + 2)

    pairs = [
        remote(slab.at[:, pl.ds(*part)], slab_in.at[:, pl.ds(*part)], pair_sems.at[0, i], pair_sems.at[1, i], partner)
        for i, part in enumerate(parts)
    ]
    for copy in pairs:
        copy.start()

    def tiles(block, table, index):
        moved = jnp.full((HALF, block.shape[1]), table[index, 2 * sub], jnp.int32) != 2 * sub
        first, second = block[:HALF, :], block[HALF:, :]
        return jnp.where(moved, second, first), jnp.where(moved, first, second)

    def extend_add(i):
        pairs[i].wait_recv()
        cols = slice(parts[i][0], sum(parts[i]))
        own = tiles(slab[:, cols], low_table, cube)
        theirs = tiles(slab_in[:, cols], low_table, cube + 1 - 2 * core)
        front[:HALF, cols] = own[0] + theirs[0]
        front[HALF:, cols] = own[1] + theirs[1]

    def p1_piece(i):
        return remote(front.at[rows(i), pl.ds(SEP, HALF)], p1.at[rows(i)], p1_cut.at[i], piece_recv.at[0], (cube, i))

    def p2_piece(i):
        return remote(front.at[rows(i, HALF), pl.ds(SEP, SEP)], p2.at[rows(i)], p2_cut.at[i], piece_recv.at[1], (cube, i))

    def lead_piece(i):
        return remote(front.at[rows(i, core * HALF)], lead.at[rows(i)], lead_cut.at[i], piece_recv.at[2], (cube, i))

    blocks = (p1, p2, lead)

    def share(n, i):
        own = blocks[n].at[rows(sub)]
        return remote(own, own, gather_send.at[n], gather_recv.at[n], (cube, i))

    def pass_on(n, owner):
        own = blocks[n].at[rows(sub)]

        @pl.when(sub != owner)
        def _():
            remote(own, own, gather_send.at[n], piece_recv.at[n], (cube, owner)).wait_recv()

        each_peer(lambda i: share(n, i).start())

    def all_shares(n):
        others = blocks[n].at[pl.ds(0, 8 * (BLOCKS - 1))]
        return remote(others, others, gather_send.at[n], gather_recv.at[n], partner)

    extend_add(0)

    @pl.when(sub == 1)
    def _():
        each_peer(lambda i: p1_piece(i).start())
        p1[rows(sub), :] = front[rows(sub), SEP : SEP + HALF]

    extend_add(1)

    @pl.when(sub == 1)
    def _():
        each_peer(lambda i: p2_piece(i).start())
        p2[rows(sub), :] = front[rows(sub, HALF), SEP:]

    extend_add(2)

    @pl.when(sub == 0)
    def _():
        each_peer(lambda i: lead_piece(i).start())
        lead[rows(sub), :] = front[rows(sub, core * HALF), :]

    pass_on(0, 1)
    pass_on(1, 1)
    pass_on(2, 0)

    all_shares(0).wait_recv()
    inv1 = inverse_factor(p1[...])
    inv[:HALF, :HALF] = inv1
    inv[:HALF, HALF:] = jnp.zeros((HALF, HALF), jnp.float32)
    all_shares(1).wait_recv()
    low = nt(p2[:, :HALF], inv1)
    inv2 = inverse_factor(p2[:, HALF:] - nt(low, low))
    inv[HALF:, HALF:] = inv2
    all_shares(2).wait_recv()
    root1 = nt(lead[:, SEP : SEP + HALF], inv1)
    root2 = nt(lead[:, SEP + HALF :] - nt(root1, low), inv2)
    root[:, :HALF] = root1
    root[:, HALF:] = root2
    root_copy = remote(root, root_in, root_sems.at[0], root_sems.at[1], partner)
    c1_copies = [
        remote(c1.at[0], c1.at[slot], c1_send.at[i], c1_recv.at[slot], device)
        for i, (slot, device) in enumerate(((0, partner), (1, across), (1, diagonal)))
    ]
    c2_copy = remote(c2.at[0], c2.at[1], c2_sems.at[0], c2_sems.at[1], across)

    @pl.when(core == 0)
    def _():
        c1[0] = lead[:, :HALF] - nt(root1, root1) - nt(root2, root2)
        for copy in reversed(c1_copies):
            copy.start()
        root_copy.start()

    @pl.when(core == 1)
    def _():
        c2[0, :, HALF:] = lead[:, HALF:SEP] - nt(root1, root1) - nt(root2, root2)
        root_copy.wait_recv()
        c2[0, :, :HALF] = lead[:, :HALF] - nt(root1, root_in[:, :HALF]) - nt(root2, root_in[:, HALF:])
        pl.when(upper == 0)(c2_copy.start)

    inv[HALF:, :HALF] = -dot(inv2, dot(low, inv1))
    keep = (sub != 1).astype(jnp.float32)
    w = dot_nt(front[:, SEP:], inv[...])
    own_columns = front[:, pl.ds(pl.multiple_of(core * HALF, HALF), HALF)]
    child[core] = (own_columns - dot_nt(w, root[...])) * keep
    mine, theirs = child.at[core], child.at[2 + core]
    child_copies = [
        (remote(mine, theirs, child_send.at[0], child_recv.at[2 + core], across), jnp.logical_or(core == 0, upper == 0)),
        (remote(mine, mine, child_send.at[1], child_recv.at[core], partner), jnp.logical_and(core == 0, upper == 0)),
        (remote(mine, theirs, child_send.at[2], child_recv.at[2 + core], diagonal), jnp.logical_and(core == 0, upper == 1)),
    ]
    for copy, wanted in child_copies:
        pl.when(wanted)(copy.start)
    panel[0] = w[:, :HALF]
    panel[1] = w[:, HALF:]
    out_low[0] = panel[core]

    pl.when(core == 1)(c1_copies[0].wait_recv)
    c1_copies[1].wait_recv()
    high1 = inverse_factor(c1[0] + c1[1])
    inv_high[...] = high1
    share_rows = pl.ds(pl.multiple_of(core * 64, 64), 64)

    def child_wait(slot):
        remote(child.at[slot], child.at[slot], child_send.at[0], child_recv.at[slot], partner).wait_recv()

    def high_columns(half):
        own = tiles(child[half], high_table, node)
        theirs = tiles(child[2 + half], high_table, other)
        return jnp.concatenate([own[0] + theirs[0], own[1] + theirs[1]], axis=0)

    q2_copy = remote(q2, q2, q2_sems.at[0], q2_sems.at[1], partner)
    high_copy = remote(high.at[core], high.at[core], high_sems.at[0], high_sems.at[1], partner)

    @pl.when(upper == 0)
    def _():
        pl.when(core == 1)(lambda: child_wait(0))
        child_wait(2)
        out_high[...] = nt(inv_high[share_rows, :], high_columns(0))

    @pl.when(upper == 1)
    def _():
        @pl.when(core == 1)
        def _():
            c2_copy.wait_recv()
            q2[...] = c2[0] + c2[1]
            q2_copy.start()

        pl.when(core == 0)(q2_copy.wait_recv)
        high_low = nt(q2[:, :HALF], high1)

        def own_high():
            child_wait(2 + core)
            high[core] = high_columns(core)
            high_copy.start()

        high2 = inverse_factor(q2[:, HALF:] - nt(high_low, high_low), HOOK, own_high)
        carried = dot(high_low, high1)
        other_half = high.at[1 - core]
        remote(other_half, other_half, high_sems.at[0], high_sems.at[1], partner).wait_recv()
        inv_high[...] = high2
        out_high[...] = nt(inv_high[share_rows, :], high[1] - nt(high[0], carried))

    for copy in pairs:
        copy.wait_send()
    for n in range(3):
        all_shares(n).wait_send()

    @pl.when(sub == 1)
    def _():
        each_peer(lambda i: p1_piece(i).wait_send())
        each_peer(lambda i: p2_piece(i).wait_send())

    @pl.when(sub == 0)
    def _():
        each_peer(lambda i: lead_piece(i).wait_send())

    @pl.when(core == 0)
    def _():
        root_copy.wait_send()
        for copy in c1_copies:
            copy.wait_send()

    @pl.when(core == 1)
    def _():
        pl.when(upper == 0)(c2_copy.wait_send)
        pl.when(upper == 1)(q2_copy.wait_send)

    pl.when(upper == 1)(high_copy.wait_send)
    for copy, wanted in child_copies:
        pl.when(wanted)(copy.wait_send)


def body(leaf_update, maps_low, maps_high):
    dma = pltpu.SemaphoreType.DMA

    def vmem(*shape):
        return pltpu.VMEM(shape, jnp.float32)

    low, high = pl.pallas_call(
        kernel,
        out_shape=(
            jax.ShapeDtypeStruct((1, SEP, HALF), jnp.float32),
            jax.ShapeDtypeStruct((HALF // 2, SEP), jnp.float32),
        ),
        in_specs=[pl.BlockSpec(memory_space=pl.ANY)] * 3,
        out_specs=(pl.BlockSpec(memory_space=pltpu.VMEM), pl.BlockSpec(memory_space=pltpu.VMEM)),
        scratch_shapes=[
            vmem(SEP, 2 * SEP), vmem(SEP, 2 * SEP), vmem(SEP, 2 * SEP),
            vmem(HALF, HALF), vmem(HALF, SEP), vmem(HALF, 2 * SEP),
            vmem(SEP, SEP), vmem(HALF, SEP), vmem(HALF, SEP), vmem(2, SEP, HALF),
            vmem(2, HALF, HALF), vmem(2, HALF, SEP), vmem(HALF, SEP), vmem(4, SEP, HALF), vmem(2, SEP, HALF),
            vmem(HALF, HALF),
            pltpu.SMEM((32, 32), jnp.int32), pltpu.SMEM((16, 32), jnp.int32), dma((2,)), dma((3,)), dma((2, 3)),
            dma((BLOCKS,)), dma((BLOCKS,)), dma((BLOCKS,)), dma((3,)), dma((3,)), dma((3,)),
            dma((2,)), dma((3,)), dma((2,)), dma((2,)), dma((2,)), dma((3,)), dma((4,)), dma((2,)),
        ],
        compiler_params=pltpu.CompilerParams(
            collective_id=0, has_side_effects=True, vmem_limit_bytes=64 * 1024 * 1024
        ),
        cost_estimate=pl.CostEstimate(flops=2_000_000_000, bytes_accessed=1_000_000, transcendentals=0),
    )(maps_low, maps_high, leaf_update)
    return low, high.T[None]


def solution(mesh):
    in_specs = (P("cube", "sub", None), P(), P())
    out_specs = (P("cube", "sub", None), P("cube", "sub", None))
    return jax.shard_map(body, mesh=mesh, in_specs=in_specs, out_specs=out_specs, check_vma=False)
```

time: 47.3 us -> 42.2 us (0.89)
  the two profiles are of different devices: /device:TPU:1 before, /device:TPU:329 now
where the time goes in v3:
time: 42.2 us; the launch traced here: 42 us
  Pallas kernels  38.3 us (91%)
  local copies, waits for them, and re-layouts  3.04 us (7%)
  between operations  0.64 us (2%)
    pallas_call x1, Pallas kernels, body(): pl.pallas_call(kernel, out_shape=(jax.ShapeDtypeStruct((1, SEP, HALF), jn...  38.3 us
    unnamed x2, local copies, waits for them, and re-layouts  3.04 us

profile of v3, /device:TPU:329, one launch (start us, length us, event | category | flops | bytes accessed | tf_op | source)
XLA Modules:
  0.0 42.0 jit_solution(20617049528065487)
XLA Ops:
  0.6 38.3 %shard_map.50 = (f32[1,256,128]{2,1,0:T(8,128)}, f32[64,256]{1,0:T(8,128)}) custom-call(s32[32,32]{1,0:T(8,128)} %maps_low.1, s32[16,32]{1,0:T(8,128)} %maps_high.1, f32[1,256,4096]{2,1,0:T(8,128)} %leaf.1), custom_call_target="tpu_custom_call" | custom-call | flops 2000000000 | bytes 1000000 | tf_op jit(solution)/shard_map/pallas_call | solution.py:396
  38.9 1.6 %copy.7 = f32[1,256,128]{2,1,0:T(8,128)} copy(f32[1,256,128]{2,1,0:T(8,128)} %get-tuple-element.8) | data formatting | bytes 262144
  40.5 1.5 %copy.8 = f32[1,256,64]{1,2,0:T(8,128)} copy(f32[1,256,64]{1,2,0:T(8,128)} %bitcast.3) | data formatting | bytes 131072

commit v4 on v3

--- a/solution.py
+++ b/solution.py
@@ -9,19 +9,17 @@
 HALF = 128
 BLOCKS = 16
 BAND = 4
-HOOK = 10
+P2_STEP = 10
+ROWS_STEP = 1
+LEAD_STEP = 8
+OWN_STEP = 11
+BOTH_STEP = 14
 HIGHEST = lax.Precision.HIGHEST
 MESH = pl.DeviceIdType.MESH
 
 
 def dot(a, b):
     return jnp.dot(a, b, precision=HIGHEST, preferred_element_type=jnp.float32)
-
-
-def dot_nt(a, b):
-    return lax.dot_general(
-        a, b, (((1,), (1,)), ((), ())), precision=HIGHEST, preferred_element_type=jnp.float32
-    )
 
 
 def pieces(x):
@@ -59,7 +57,7 @@
     return (x.reshape(n // 8, 8, HALF) * r[None]).reshape(n, HALF)
 
 
-def inverse_factor(block, hook_at=None, hook=None):
+def inverse_factor(block, hooks=None):
     n = block.shape[0]
     steps = n // 8
     sublane = lax.broadcasted_iota(jnp.int32, (8, HALF), 0)
@@ -72,8 +70,8 @@
     done = []
     head = [lane(trail[:8], j) for j in range(8)]
     for k in range(steps):
-        if hook is not None and k == hook_at:
-            hook()
+        if hooks and k in hooks:
+            hooks[k]()
         c0 = 8 * k
         t_head, t_tail = trail[:8], trail[8:]
         u_head, u_tail = unit[:8], unit[8:]
@@ -86,15 +84,10 @@
         pivots = None
         for j in range(8):
             pivot = row(head[j], j)
-            if j % 2 == 0:
-                inv = 1.0 / pivot
-                beside = row(head[j + 1], j)
-                inv_next = pivot * (1.0 / (pivot * row(head[j + 1], j + 1) - beside * beside))
-            else:
-                inv = inv_next
+            inv = 1.0 / pivot
             head_inv = head[j] * inv
             for q in range(j + 1, 8):
-                m = row(head[q], j) * inv if q <= j + 2 else row(head_inv, q)
+                m = row(head[q], j) * inv if q == j + 1 else row(head_inv, q)
                 head[q] = head[q] - head[j] * m
                 if not last:
                     tail[q] = tail[q] - scaled(tail[j], m)
@@ -133,9 +126,9 @@
 
 def kernel(
     maps_low, maps_high, leaf, out_low, out_high,
-    slab, slab_in, front, p1, p2, lead, inv, root, root_in, panel, c1, c2, q2, child, high, inv_high,
+    slab, slab_in, front, p1_stage, p1, p2, lead, root, root_in, panel, c1, c2, q2, child, high, inv_high, left, pending, result,
     low_table, high_table, table_sems, load_sems, pair_sems,
-    p1_cut, p2_cut, lead_cut, gather_send, gather_recv, piece_recv,
+    p1_cut, p2_cut, lead_cut, gather_send, gather_recv, piece_recv, stage_recv, p2_pair, out_sems,
     root_sems, c1_send, c1_recv, c2_sems, q2_sems, child_send, child_recv, high_sems,
 ):
     cube = lax.axis_index("cube")
@@ -183,16 +176,36 @@
     for device in (partner, across, diagonal):
         greet(device)
     each_peer(lambda i: greet((cube, i)))
-    for copy in tables + loads:
-        copy.wait()
-    pl.semaphore_wait(barrier, BLOCKS + 2)
+    pl.when(sub != 1)(lambda: greet((partner[0], 1)))
+    pl.when(sub != 1)(lambda: pl.semaphore_wait(barrier, BLOCKS + 2))
+    pl.when(sub == 1)(lambda: pl.semaphore_wait(barrier, 2 * BLOCKS + 1))
+
+    def p1_piece(cube_to, i):
+        return remote(slab.at[rows(i), pl.ds(SEP, HALF)], p1_stage.at[core], p1_cut, stage_recv.at[core], (cube_to, i))
+
+    loads[0].wait()
+
+    @pl.when(sub == 1)
+    def _():
+        def both(i):
+            p1_piece(cube, i).start()
+            p1_piece(partner[0], i).start()
+
+        each_peer(both)
+        p1_piece(partner[0], sub).start()
+        p1_stage[core] = slab[rows(sub), SEP : SEP + HALF]
+
 
     pairs = [
         remote(slab.at[:, pl.ds(*part)], slab_in.at[:, pl.ds(*part)], pair_sems.at[0, i], pair_sems.at[1, i], partner)
         for i, part in enumerate(parts)
     ]
-    for copy in pairs:
+    pairs[0].start()
+    for load, copy in zip(loads[1:], pairs[1:]):
+        load.wait()
         copy.start()
+    for copy in tables:
+        copy.wait()
 
     def tiles(block, table, index):
         moved = jnp.full((HALF, block.shape[1]), table[index, 2 * sub], jnp.int32) != 2 * sub
@@ -207,16 +220,15 @@
         front[:HALF, cols] = own[0] + theirs[0]
         front[HALF:, cols] = own[1] + theirs[1]
 
-    def p1_piece(i):
-        return remote(front.at[rows(i), pl.ds(SEP, HALF)], p1.at[rows(i)], p1_cut.at[i], piece_recv.at[0], (cube, i))
+    p2_columns = pl.ds(pl.multiple_of(SEP + core * HALF, HALF), HALF)
 
     def p2_piece(i):
-        return remote(front.at[rows(i, HALF), pl.ds(SEP, SEP)], p2.at[rows(i)], p2_cut.at[i], piece_recv.at[1], (cube, i))
+        return remote(front.at[rows(i, HALF), p2_columns], p2.at[core, rows(i)], p2_cut.at[i], piece_recv.at[1], (cube, i))
 
     def lead_piece(i):
         return remote(front.at[rows(i, core * HALF)], lead.at[rows(i)], lead_cut.at[i], piece_recv.at[2], (cube, i))
 
-    blocks = (p1, p2, lead)
+    blocks = (p1, p2.at[core], lead)
 
     def share(n, i):
         own = blocks[n].at[rows(sub)]
@@ -236,18 +248,12 @@
         return remote(others, others, gather_send.at[n], gather_recv.at[n], partner)
 
     extend_add(0)
+    extend_add(1)
 
     @pl.when(sub == 1)
     def _():
-        each_peer(lambda i: p1_piece(i).start())
-        p1[rows(sub), :] = front[rows(sub), SEP : SEP + HALF]
-
-    extend_add(1)
-
-    @pl.when(sub == 1)
-    def _():
         each_peer(lambda i: p2_piece(i).start())
-        p2[rows(sub), :] = front[rows(sub, HALF), SEP:]
+        p2[core, rows(sub), :] = front[rows(sub, HALF), p2_columns]
 
     extend_add(2)
 
@@ -256,49 +262,80 @@
         each_peer(lambda i: lead_piece(i).start())
         lead[rows(sub), :] = front[rows(sub, core * HALF), :]
 
-    pass_on(0, 1)
+    for c in range(2):
+        @pl.when(jnp.logical_or(sub != 1, core != c))
+        def _():
+            remote(p1_stage.at[c], p1_stage.at[c], p1_cut, stage_recv.at[c], partner).wait_recv()
+
+    p1[rows(sub), :] = p1_stage[0] + p1_stage[1]
+    each_peer(lambda i: share(0, i).start())
     pass_on(1, 1)
     pass_on(2, 0)
 
     all_shares(0).wait_recv()
-    inv1 = inverse_factor(p1[...])
-    inv[:HALF, :HALF] = inv1
-    inv[:HALF, HALF:] = jnp.zeros((HALF, HALF), jnp.float32)
-    all_shares(1).wait_recv()
-    low = nt(p2[:, :HALF], inv1)
-    inv2 = inverse_factor(p2[:, HALF:] - nt(low, low))
-    inv[HALF:, HALF:] = inv2
-    all_shares(2).wait_recv()
-    root1 = nt(lead[:, SEP : SEP + HALF], inv1)
-    root2 = nt(lead[:, SEP + HALF :] - nt(root1, low), inv2)
-    root[:, :HALF] = root1
+    p2_copy = remote(p2.at[core], p2.at[core], p2_pair.at[0], p2_pair.at[1], partner)
+
+    def p2_half():
+        all_shares(1).wait_recv()
+        p2_copy.start()
+
+    inv1 = inverse_factor(p1[...], {P2_STEP: p2_half})
+    p2_other = p2.at[1 - core]
+    remote(p2_other, p2_other, p2_pair.at[0], p2_pair.at[1], partner).wait_recv()
+    low = nt(p2[0], inv1)
+    root_copies = [
+        remote(root.at[:, part], root_in.at[:, part], root_sems.at[0, i], root_sems.at[1, i], partner)
+        for i, part in enumerate((pl.ds(0, HALF), pl.ds(HALF, HALF)))
+    ]
+
+    def first_root():
+        all_shares(2).wait_recv()
+        root1 = nt(lead[:, SEP : SEP + HALF], inv1)
+        root[:, :HALF] = root1
+        pl.when(core == 0)(root_copies[0].start)
+        left[0] = lead[:, SEP + HALF :] - nt(root1, low)
+        left[1] = lead[:, pl.ds(pl.multiple_of(core * HALF, HALF), HALF)] - nt(root1, root1)
+
+        child[core] = own_columns - nt(panel[0], root1)
+
+    own_columns = front[:, pl.ds(pl.multiple_of(core * HALF, HALF), HALF)]
+
+    def first_panel():
+        panel[0] = nt(front[:, SEP : SEP + HALF], inv1)
+        panel[1] = front[:, SEP + HALF :] - nt(panel[0], low)
+
+    inv2 = inverse_factor(p2[1] - nt(low, low), {ROWS_STEP: first_panel, LEAD_STEP: first_root})
+    root2 = nt(left[0], inv2)
     root[:, HALF:] = root2
-    root_copy = remote(root, root_in, root_sems.at[0], root_sems.at[1], partner)
     c1_copies = [
         remote(c1.at[0], c1.at[slot], c1_send.at[i], c1_recv.at[slot], device)
         for i, (slot, device) in enumerate(((0, partner), (1, across), (1, diagonal)))
     ]
-    c2_copy = remote(c2.at[0], c2.at[1], c2_sems.at[0], c2_sems.at[1], across)
+    c2_copies = [
+        remote(c2.at[0, part], c2.at[1, part], c2_sems.at[0, part], c2_sems.at[1, part], across) for part in range(2)
+    ]
 
     @pl.when(core == 0)
     def _():
-        c1[0] = lead[:, :HALF] - nt(root1, root1) - nt(root2, root2)
+        root_copies[1].start()
+        c1[0] = left[1] - nt(root2, root2)
         for copy in reversed(c1_copies):
             copy.start()
-        root_copy.start()
 
     @pl.when(core == 1)
     def _():
-        c2[0, :, HALF:] = lead[:, HALF:SEP] - nt(root1, root1) - nt(root2, root2)
-        root_copy.wait_recv()
-        c2[0, :, :HALF] = lead[:, :HALF] - nt(root1, root_in[:, :HALF]) - nt(root2, root_in[:, HALF:])
-        pl.when(upper == 0)(c2_copy.start)
-
-    inv[HALF:, :HALF] = -dot(inv2, dot(low, inv1))
+        c2[0, 1] = left[1] - nt(root2, root2)
+        pl.when(upper == 0)(c2_copies[1].start)
+        root_copies[0].wait_recv()
+        across1 = nt(root[:, :HALF], root_in[:, :HALF])
+        root_copies[1].wait_recv()
+        c2[0, 0] = lead[:, :HALF] - across1 - nt(root2, root_in[:, HALF:])
+        pl.when(upper == 0)(c2_copies[0].start)
+
     keep = (sub != 1).astype(jnp.float32)
-    w = dot_nt(front[:, SEP:], inv[...])
-    own_columns = front[:, pl.ds(pl.multiple_of(core * HALF, HALF), HALF)]
-    child[core] = (own_columns - dot_nt(w, root[...])) * keep
+    w2 = nt(panel[1], inv2)
+    panel[1] = w2
+    child[core] = (child[core] - nt(w2, root2)) * keep
     mine, theirs = child.at[core], child.at[2 + core]
     child_copies = [
         (remote(mine, theirs, child_send.at[0], child_recv.at[2 + core], across), jnp.logical_or(core == 0, upper == 0)),
@@ -307,9 +344,11 @@
     ]
     for copy, wanted in child_copies:
         pl.when(wanted)(copy.start)
-    panel[0] = w[:, :HALF]
-    panel[1] = w[:, HALF:]
-    out_low[0] = panel[core]
+    out_copies = [
+        pltpu.make_async_copy(panel.at[core], out_low.at[0], out_sems.at[0]),
+        pltpu.make_async_copy(result, out_high, out_sems.at[1]),
+    ]
+    out_copies[0].start()
 
     pl.when(core == 1)(c1_copies[0].wait_recv)
     c1_copies[1].wait_recv()
@@ -325,46 +364,58 @@
         theirs = tiles(child[2 + half], high_table, other)
         return jnp.concatenate([own[0] + theirs[0], own[1] + theirs[1]], axis=0)
 
-    q2_copy = remote(q2, q2, q2_sems.at[0], q2_sems.at[1], partner)
+    q2_copies = [remote(q2.at[part], q2.at[part], q2_sems.at[0, part], q2_sems.at[1, part], partner) for part in range(2)]
     high_copy = remote(high.at[core], high.at[core], high_sems.at[0], high_sems.at[1], partner)
 
     @pl.when(upper == 0)
     def _():
         pl.when(core == 1)(lambda: child_wait(0))
         child_wait(2)
-        out_high[...] = nt(inv_high[share_rows, :], high_columns(0))
+        result[...] = nt(inv_high[share_rows, :], high_columns(0))
 
     @pl.when(upper == 1)
     def _():
         @pl.when(core == 1)
         def _():
-            c2_copy.wait_recv()
-            q2[...] = c2[0] + c2[1]
-            q2_copy.start()
-
-        pl.when(core == 0)(q2_copy.wait_recv)
-        high_low = nt(q2[:, :HALF], high1)
+            for part in (1, 0):
+                c2_copies[part].wait_recv()
+                q2[part] = c2[0, part] + c2[1, part]
+                q2_copies[part].start()
+
+        @pl.when(core == 0)
+        def _():
+            for part in (1, 0):
+                q2_copies[part].wait_recv()
+
+        high_low = nt(q2[0], high1)
 
         def own_high():
             child_wait(2 + core)
             high[core] = high_columns(core)
             high_copy.start()
 
-        high2 = inverse_factor(q2[:, HALF:] - nt(high_low, high_low), HOOK, own_high)
         carried = dot(high_low, high1)
         other_half = high.at[1 - core]
-        remote(other_half, other_half, high_sems.at[0], high_sems.at[1], partner).wait_recv()
+
+        def both_high():
+            remote(other_half, other_half, high_sems.at[0], high_sems.at[1], partner).wait_recv()
+            pending[...] = high[1] - nt(high[0], carried)
+
+        high2 = inverse_factor(q2[1] - nt(high_low, high_low), {OWN_STEP: own_high, BOTH_STEP: both_high})
         inv_high[...] = high2
-        out_high[...] = nt(inv_high[share_rows, :], high[1] - nt(high[0], carried))
-
-    for copy in pairs:
+        result[...] = nt(inv_high[share_rows, :], pending[...])
+
+    out_copies[1].start()
+
+    for copy in (*pairs, p2_copy):
         copy.wait_send()
     for n in range(3):
         all_shares(n).wait_send()
 
     @pl.when(sub == 1)
     def _():
-        each_peer(lambda i: p1_piece(i).wait_send())
+        sent = slab_in.at[pl.ds(0, 8 * (2 * BLOCKS - 1)), pl.ds(0, HALF)]
+        remote(sent, sent, p1_cut, stage_recv.at[0], partner).wait_send()
         each_peer(lambda i: p2_piece(i).wait_send())
 
     @pl.when(sub == 0)
@@ -373,18 +424,27 @@
 
     @pl.when(core == 0)
     def _():
-        root_copy.wait_send()
+        for copy in root_copies:
+            copy.wait_send()
         for copy in c1_copies:
             copy.wait_send()
 
     @pl.when(core == 1)
     def _():
-        pl.when(upper == 0)(c2_copy.wait_send)
-        pl.when(upper == 1)(q2_copy.wait_send)
+        for part in range(2):
+            pl.when(upper == 0)(c2_copies[part].wait_send)
+            pl.when(upper == 1)(q2_copies[part].wait_send)
 
     pl.when(upper == 1)(high_copy.wait_send)
     for copy, wanted in child_copies:
         pl.when(wanted)(copy.wait_send)
+    for copy in out_copies:
+        copy.wait()
+
+
+def place(low, high, out_low, out_high):
+    out_low[...] = low[...]
+    out_high[...] = high[...]
 
 
 def body(leaf_update, maps_low, maps_high):
@@ -400,22 +460,28 @@
             jax.ShapeDtypeStruct((HALF // 2, SEP), jnp.float32),
         ),
         in_specs=[pl.BlockSpec(memory_space=pl.ANY)] * 3,
-        out_specs=(pl.BlockSpec(memory_space=pltpu.VMEM), pl.BlockSpec(memory_space=pltpu.VMEM)),
+        out_specs=(pl.BlockSpec(memory_space=pl.ANY),) * 2,
         scratch_shapes=[
             vmem(SEP, 2 * SEP), vmem(SEP, 2 * SEP), vmem(SEP, 2 * SEP),
-            vmem(HALF, HALF), vmem(HALF, SEP), vmem(HALF, 2 * SEP),
-            vmem(SEP, SEP), vmem(HALF, SEP), vmem(HALF, SEP), vmem(2, SEP, HALF),
-            vmem(2, HALF, HALF), vmem(2, HALF, SEP), vmem(HALF, SEP), vmem(4, SEP, HALF), vmem(2, SEP, HALF),
-            vmem(HALF, HALF),
+            vmem(2, 8, HALF), vmem(HALF, HALF), vmem(2, HALF, HALF), vmem(HALF, 2 * SEP),
+            vmem(HALF, SEP), vmem(HALF, SEP), vmem(2, SEP, HALF),
+            vmem(2, HALF, HALF), vmem(2, 2, HALF, HALF), vmem(2, HALF, HALF), vmem(4, SEP, HALF), vmem(2, SEP, HALF),
+            vmem(HALF, HALF), vmem(2, HALF, HALF), vmem(SEP, HALF), vmem(HALF // 2, SEP),
             pltpu.SMEM((32, 32), jnp.int32), pltpu.SMEM((16, 32), jnp.int32), dma((2,)), dma((3,)), dma((2, 3)),
-            dma((BLOCKS,)), dma((BLOCKS,)), dma((BLOCKS,)), dma((3,)), dma((3,)), dma((3,)),
-            dma((2,)), dma((3,)), dma((2,)), dma((2,)), dma((2,)), dma((3,)), dma((4,)), dma((2,)),
+            dma, dma((BLOCKS,)), dma((BLOCKS,)), dma((3,)), dma((3,)), dma((3,)), dma((2,)), dma((2,)), dma((2,)),
+            dma((2, 2)), dma((3,)), dma((2,)), dma((2, 2)), dma((2, 2)), dma((3,)), dma((4,)), dma((2,)),
         ],
         compiler_params=pltpu.CompilerParams(
             collective_id=0, has_side_effects=True, vmem_limit_bytes=64 * 1024 * 1024
         ),
         cost_estimate=pl.CostEstimate(flops=2_000_000_000, bytes_accessed=1_000_000, transcendentals=0),
     )(maps_low, maps_high, leaf_update)
+    low, high = pl.pallas_call(
+        place,
+        out_shape=(jax.ShapeDtypeStruct(low.shape, low.dtype), jax.ShapeDtypeStruct(high.shape, high.dtype)),
+        in_specs=[pl.BlockSpec(memory_space=pltpu.VMEM)] * 2,
+        out_specs=(pl.BlockSpec(memory_space=pltpu.VMEM),) * 2,
+    )(low, high)
     return low, high.T[None]
 
 

time: 42.2 us -> 40.2 us (0.953)
  local copies, waits for them, and re-layouts: 3.04 us -> 0 us
  Pallas kernels: 38.3 us -> 39.4 us
    unnamed x2 -> x0, local copies, waits for them, and re-layouts: 3.04 us -> none
    pallas_call x0 -> x1, Pallas kernels: none -> 1.59 us  [body(): pl.pallas_call(place, out_shape=(jax.ShapeDtypeStruct(low.shape, low.dtyp...]
    pallas_call x1, Pallas kernels: 38.3 us -> 37.8 us  [body(): pl.pallas_call(kernel, out_shape=(jax.ShapeDtypeStruct((1, SEP, HALF), jn...]
where the time goes in v4:
time: 40.2 us; the launch traced here: 40 us
  Pallas kernels  39.4 us (98%)
  between operations  0.64 us (2%)
    pallas_call x1, Pallas kernels, body(): pl.pallas_call(kernel, out_shape=(jax.ShapeDtypeStruct((1, SEP, HALF), jn...  37.8 us
    pallas_call x1, Pallas kernels, body(): pl.pallas_call(place, out_shape=(jax.ShapeDtypeStruct(low.shape, low.dtyp...  1.59 us

profile of v4, /device:TPU:329, one launch (start us, length us, event | category | flops | bytes accessed | tf_op | source)
XLA Modules:
  0.0 40.0 jit_solution(10561428441573343861)
XLA Ops:
  0.6 37.8 %shard_map.50 = (f32[1,256,128]{2,1,0:T(8,128)}, f32[64,256]{1,0:T(8,128)}) custom-call(s32[32,32]{1,0:T(8,128)} %maps_low.1, s32[16,32]{1,0:T(8,128)} %maps_high.1, f32[1,256,4096]{2,1,0:T(8,128)} %leaf.1), custom_call_target="tpu_custom_call" | custom-call | flops 2000000000 | bytes 1000000 | tf_op jit(solution)/shard_map/pallas_call | solution.py:456
  38.4 1.6 %shard_map.51 = (f32[1,256,128]{2,1,0:T(8,128)}, f32[64,256]{1,0:T(8,128)}) custom-call(f32[1,256,128]{2,1,0:T(8,128)} %get-tuple-element.6.low, f32[64,256]{1,0:T(8,128)} %get-tuple-element.7.high), custom_call_target="tpu_custom_call" | custom-call | tf_op jit(solution)/shard_map/pallas_call | solution.py:479

commit v5 on v4

--- a/solution.py
+++ b/solution.py
@@ -9,11 +9,11 @@
 HALF = 128
 BLOCKS = 16
 BAND = 4
-P2_STEP = 10
+P2_STEP = 13
 ROWS_STEP = 1
-LEAD_STEP = 8
-OWN_STEP = 11
-BOTH_STEP = 14
+LEAD_STEP = 10
+OWN_STEP = 13
+BOTH_STEP = 15
 HIGHEST = lax.Precision.HIGHEST
 MESH = pl.DeviceIdType.MESH
 
@@ -114,9 +114,9 @@
         if k % BAND == BAND - 1 and far is not None:
             top = n - far.shape[0]
             rows_done = jnp.concatenate(band_rows, axis=0)
-            ahead_rows = rows_done[:, top:]
-            far = far - stacked(ahead_rows, rows_done, 0, 0)
-            far_unit = far_unit - stacked(ahead_rows, jnp.concatenate(band_unit, axis=0), 0, 0)
+            both = jnp.concatenate([rows_done, jnp.concatenate(band_unit, axis=0)], axis=1)
+            change = stacked(rows_done, both, 0, 0)[top:]
+            far, far_unit = far - change[:, :n], far_unit - change[:, n:]
             take = min(8 * BAND, n - top)
             trail = jnp.concatenate([trail, far[:take]], axis=0)
             unit = jnp.concatenate([unit, far_unit[:take]], axis=0)

time: 40.2 us -> 39.7 us (0.988)
  Pallas kernels: 39.4 us -> 38.9 us
    pallas_call x1, Pallas kernels: 37.8 us -> 37.3 us  [body(): pl.pallas_call(kernel, out_shape=(jax.ShapeDtypeStruct((1, SEP, HALF), jn...]
where the time goes in v5:
time: 39.7 us; the launch traced here: 39.6 us
  Pallas kernels  38.9 us (98%)
  between operations  0.64 us (2%)
    pallas_call x1, Pallas kernels, body(): pl.pallas_call(kernel, out_shape=(jax.ShapeDtypeStruct((1, SEP, HALF), jn...  37.3 us
    pallas_call x1, Pallas kernels, body(): pl.pallas_call(place, out_shape=(jax.ShapeDtypeStruct(low.shape, low.dtyp...  1.59 us

profile of v5, /device:TPU:329, one launch (start us, length us, event | category | flops | bytes accessed | tf_op | source)
XLA Modules:
  0.0 39.6 jit_solution(4389905444036051452)
XLA Ops:
  0.6 37.3 %shard_map.50 = (f32[1,256,128]{2,1,0:T(8,128)}, f32[64,256]{1,0:T(8,128)}) custom-call(s32[32,32]{1,0:T(8,128)} %maps_low.1, s32[16,32]{1,0:T(8,128)} %maps_high.1, f32[1,256,4096]{2,1,0:T(8,128)} %leaf.1), custom_call_target="tpu_custom_call" | custom-call | flops 2000000000 | bytes 1000000 | tf_op jit(solution)/shard_map/pallas_call | solution.py:456
  38.0 1.6 %shard_map.51 = (f32[1,256,128]{2,1,0:T(8,128)}, f32[64,256]{1,0:T(8,128)}) custom-call(f32[1,256,128]{2,1,0:T(8,128)} %get-tuple-element.6.low, f32[64,256]{1,0:T(8,128)} %get-tuple-element.7.high), custom_call_target="tpu_custom_call" | custom-call | tf_op jit(solution)/shard_map/pallas_call | solution.py:479

commit v6 on v5

--- a/solution.py
+++ b/solution.py
@@ -187,11 +187,8 @@
 
     @pl.when(sub == 1)
     def _():
-        def both(i):
-            p1_piece(cube, i).start()
-            p1_piece(partner[0], i).start()
-
-        each_peer(both)
+        each_peer(lambda i: p1_piece(cube, i).start())
+        each_peer(lambda i: p1_piece(partner[0], i).start())
         p1_piece(partner[0], sub).start()
         p1_stage[core] = slab[rows(sub), SEP : SEP + HALF]
 

time: 39.7 us -> 39.5 us (level)
  the two profiles are of different devices: /device:TPU:329 before, /device:TPU:321 now
where the time goes in v6:
time: 39.5 us; the launch traced here: 39.4 us
  Pallas kernels  38.7 us (98%)
  between operations  0.64 us (2%)
    pallas_call x1, Pallas kernels, body(): pl.pallas_call(kernel, out_shape=(jax.ShapeDtypeStruct((1, SEP, HALF), jn...  37.1 us
    pallas_call x1, Pallas kernels, body(): pl.pallas_call(place, out_shape=(jax.ShapeDtypeStruct(low.shape, low.dtyp...  1.59 us

profile of v6, /device:TPU:321, one launch (start us, length us, event | category | flops | bytes accessed | tf_op | source)
XLA Modules:
  0.0 39.4 jit_solution(3847286759006828558)
XLA Ops:
  0.6 37.1 %shard_map.50 = (f32[1,256,128]{2,1,0:T(8,128)}, f32[64,256]{1,0:T(8,128)}) custom-call(s32[32,32]{1,0:T(8,128)} %maps_low.1, s32[16,32]{1,0:T(8,128)} %maps_high.1, f32[1,256,4096]{2,1,0:T(8,128)} %leaf.1), custom_call_target="tpu_custom_call" | custom-call | flops 2000000000 | bytes 1000000 | tf_op jit(solution)/shard_map/pallas_call | solution.py:453
  37.8 1.6 %shard_map.51 = (f32[1,256,128]{2,1,0:T(8,128)}, f32[64,256]{1,0:T(8,128)}) custom-call(f32[1,256,128]{2,1,0:T(8,128)} %get-tuple-element.6.low, f32[64,256]{1,0:T(8,128)} %get-tuple-element.7.high), custom_call_target="tpu_custom_call" | custom-call | tf_op jit(solution)/shard_map/pallas_call | solution.py:476
